TPU v7x, 32 devices: a whole 2x2x4 slice. The times are simulated.
32 devices in a mesh: dp: 8 (over y, x, core), fsdp: 4 (over z).
Axes of the slice: x: 2, y: 2, z: 4, core: 2. Of those that a mesh axis runs over, the one named last changes fastest.
Arguments:
- tokens: bfloat16 [128, 256, 384], P(('dp', 'fsdp')), may hold values from -4 to 4, as said below
- cond: bfloat16 [128, 384], P(('dp', 'fsdp')), may hold values from -4 to 4, as said below
- cotangent: bfloat16 [128, 256, 384], P(('dp', 'fsdp')), may hold values from -4 to 4, as said below
- keep_mask: int32 [128], P(('dp', 'fsdp')), may hold values 0 or 1
- w_ada: bfloat16 [2, 384, 2304], P(None, 'fsdp'), may hold values from -0.20412415 to 0.20412415, as said below
- w_qkv: bfloat16 [2, 384, 1152], P(None, 'fsdp'), may hold values from -0.20412415 to 0.20412415, as said below
- w_proj: bfloat16 [2, 384, 384], P(None, 'fsdp'), may hold values from -1.6329932 to 1.6329932, as said below
- w_up: bfloat16 [2, 384, 1536], P(None, 'fsdp'), may hold values from -0.20412415 to 0.20412415, as said below
- w_down: bfloat16 [2, 1536, 384], P(None, 'fsdp'), may hold values from -0.102062073 to 0.102062073, as said below
Outputs:
- output: bfloat16 [128, 256, 384], P(('dp', 'fsdp'))
- grad_tokens: float32 [128, 256, 384], P(('dp', 'fsdp'))
- grad_cond: float32 [128, 384], P(('dp', 'fsdp'))
- grad_ada: float32 [2, 384, 2304], P(None, 'fsdp')
- grad_qkv: float32 [2, 384, 1152], P(None, 'fsdp')
- grad_proj: float32 [2, 384, 384], P(None, 'fsdp')
- grad_up: float32 [2, 384, 1536], P(None, 'fsdp')
- grad_down: float32 [2, 1536, 384], P(None, 'fsdp')
Inputs may be any that keep to these rules, and one draw needn't show every extreme that they name: `tokens`: independent entries of mean zero and deviation one. `cond`: independent entries of mean zero and deviation one. `cotangent`: independent entries of mean zero and deviation one. `w_ada`: independent entries of mean zero and deviation 384^-0.5. `w_qkv`: independent entries of mean zero and deviation 384^-0.5. `w_proj`: independent entries of mean zero. `w_up`: independent entries of mean zero and deviation 384^-0.5. `w_down`: independent entries of mean zero and deviation 1536^-0.5.
All inputs are finite; a program needn't handle non-finite values. No bound on the sum of `keep_mask` on one device may be relied on, other than what follows from the above.
Results may differ from a plain program's by a relative error of at most 0.014.
Values may be sent and summed in bfloat16 or wider, within the bound.
A program may use at most 192 MiB of HBM per device.

v0:
```python
import functools

import jax
import jax.numpy as jnp
from jax import lax
from jax.experimental import pallas as pl
from jax.experimental.pallas import tpu as pltpu
from jax.sharding import PartitionSpec as P

MESH = pl.DeviceIdType.MESH
bf, f32 = jnp.bfloat16, jnp.float32
HEADS = 6
PAIRS = HEADS // 2
GROUP = 8
NN = (((1,), (0,)), ((), ()))
NT = (((1,), (1,)), ((), ()))
TN = (((0,), (0,)), ((), ()))
GELU_A = 0.7978845608028654
GELU_B = GELU_A * 0.044715
KINDS = ("u", "d", "q0", "q1", "q2")
SPLIT = ((0, "d"), (1, "d"))
DIRECT = ((0, "d"), (0, "q"), (0, "u"), (1, "d"))
STEPS = ()
ONE = ((0, "q1"),)
METHOD = (
    {"u": "q", "d": "steps", "q0": "ring", "q1": "steps", "q2": "q"},
    {"u": "q", "d": "q", "q0": "steps", "q1": "steps", "q2": "q"},
)


def dot(a, b, dims=NN):
    return lax.dot_general(a, b, dims, preferred_element_type=f32)


def exact_dot(a, b, dims=NN):
    return lax.dot_general(a, b, dims, precision=lax.Precision.HIGHEST, preferred_element_type=f32)


def one_hot(shape, hit):
    r = lax.broadcasted_iota(jnp.int32, shape, 0)
    c = lax.broadcasted_iota(jnp.int32, shape, 1)
    return jnp.where(hit(r, c), 1.0, 0.0)


def norm_hat(v):
    c = v - jnp.mean(v, -1, keepdims=True)
    r = lax.rsqrt(jnp.mean(c * c, -1, keepdims=True) + 1e-6)
    return c * r, r


def norm_back(dx, hat, r):
    return r * (dx - jnp.mean(dx, -1, keepdims=True) - hat * jnp.mean(dx * hat, -1, keepdims=True))


def gelu_parts(x):
    x2 = x * x
    t = jnp.tanh(x * (GELU_A + GELU_B * x2))
    up = 0.5 * t + 0.5
    a = x * up
    return a, a * (1.0 - t) * (GELU_A + (3 * GELU_B) * x2) + up


class Refs:
    pass


def scratch(F, I, L, D, FF, B):
    T = I * L
    R = D // F // 2
    W = D // PAIRS
    shapes = dict(
        wq=((B, F, 2, R, FF), bf),
        wu=((B, F, 2, R, FF), bf),
        wd=((B, F, 4, 2, R, D), bf),
        wa=((B, D // F, 6 * D), bf),
        xs=((B + 1, T, D), f32),
        fi=((B, T, D), bf),
        qkv=((B, T, 3 * D), bf),
        pt=((B, I * HEADS, L, L), bf),
        mt=((B, D, T), bf),
        att=((B, T, D), bf),
        mid=((B, T, D), f32),
        si=((B, T, D), bf),
        hid=((B, T, FF), bf),
        br=((B, T, D), bf),
        db=((T, D), bf),
        act=((T, FF), bf),
        da=((T, D), bf),
        mod=((B * 3, 2 * I, D), f32),
        dm=((B, 4 * I, D), f32),
        dl=((B, 2 * I, D), f32),
        cd=((I, D), bf),
        gc=((8, D), f32),
        ms=((F, B * 6 * I, D), bf),
        mr=((F, B * 6 * I, D), bf),
        cz=((F, 16, D), bf),
        cg=((4, 2, 16, D), bf),
        dg=((B + 1, 4, 2, F, 16, D), bf),
        cs=((F, 8, D), f32),
        cr=((F, 8, D), f32),
        gq=((PAIRS, F, 2, R, 4 * W), bf),
        gu=((F, 2, R, FF), bf),
        gd=((F, 4, 2, R, D), bf),
        hq=((B, PAIRS, F, R, 4 * W), bf),
        hu=((B, F, R, FF), bf),
        hd=((B, F, 4, R, D), bf),
        oq=((B, PAIRS, 2, R, 4 * W), bf),
        ou=((B, 2, R, FF), bf),
        od=((B, 4, 2, R, D), bf),
    )
    for block in range(B):
        for w in KINDS:
            n = W if w[0] == "q" else D
            four = (4, R, n) if w == "d" else (R, 4 * n)
            at = f"{w}{block}"
            if METHOD[block][w] == "direct":
                shapes["a" + at] = ((4 * F, R, n), bf)
            elif METHOD[block][w] == "ring":
                shapes["t" + at] = (four, bf)
                shapes["a" + at] = ((2, *four), bf)
                shapes["s" + at] = (four, bf)
                shapes["b" + at] = ((3, R, n), bf)
            else:
                if METHOD[block][w] == "steps":
                    shapes["t" + at] = ((2, F, R, n), bf)
                    shapes["a" + at] = ((F, R, n), bf)
                else:
                    shapes["a" + at] = ((3, F, R, n), bf)
                shapes["s" + at] = ((F, R, n), bf)
                shapes["b" + at] = ((F, R, n), bf)
    return shapes


INPUTS = ("tokens", "cond", "cotangent", "mask", "ada", "qkv_w", "proj_w", "up_w", "down_w")
OUTPUTS = ("output", "grad_tokens", "grad_cond", "grad_ada", "grad_q", "grad_u", "grad_d")
N_SEMS = 256
N_LOCAL = 64


def kernel(names, F, I, L, D, FF, B, *refs):
    n_in, n_out = len(INPUTS), len(OUTPUTS)
    inp, out, k = Refs(), Refs(), Refs()
    for name, ref in zip(INPUTS, refs[:n_in]):
        setattr(inp, name, ref)
    for name, ref in zip(OUTPUTS, refs[n_in : n_in + n_out]):
        setattr(out, name, ref)
    for name, ref in zip(names, refs[n_in + n_out :]):
        setattr(k, name, ref)
    sems, local_sems = refs[-2], refs[-1]
    T = I * L
    R = D // F // 2
    W = D // PAIRS
    HS = D // HEADS
    images = range(I)

    me, f = lax.axis_index("dp"), lax.axis_index("fsdp")
    e = me % GROUP
    base = me - e
    c, q = e % 2, e // 2
    other = 1 - c
    z_peer = [(f + r) % F for r in range(F)]
    q_peer = [(q + j) % 4 for j in range(4)]

    def at_z(r):
        return (me, z_peer[r])

    x_next, y_next = q + 1 - 2 * (q % 2), (q + 2) % 4
    first = x_next * other + y_next * c
    second = x_next * c + y_next * other
    across = 6 - q - first - second

    def at(qi):
        return (base + 2 * qi + c, f)

    def at_q(j, r=0):
        return (base + 2 * q_peer[j] + c, z_peer[r])

    def at_c(j=0):
        return (base + 2 * q_peer[j] + other, f)

    def rows(i):
        return slice(i * L, (i + 1) * L)

    def cut(j, n):
        return pl.ds(pl.multiple_of(j * n, n), n)

    index = {}

    def sem(key):
        return sems.at[index.setdefault(key, len(index))]

    def send(key, src, dst, to):
        pltpu.make_async_remote_copy(
            src_ref=src,
            dst_ref=dst,
            send_sem=sem(("send",) + key),
            recv_sem=sem(("recv",) + key),
            device_id=to,
            device_id_type=MESH,
        ).start()

    unsent = []

    def wait(kind, key, like):
        if kind == "recv" and key[0] != "gc":
            unsent.append((key, like))
        done(kind, key, like)

    def done(kind, key, like):
        ref = like() if callable(like) else like
        pltpu.make_async_copy(ref, ref, sem((kind,) + key)).wait()

    def all_sent():
        while unsent:
            done("send", *unsent.pop(0))

    local_index = {}

    def local(key, src, dst):
        n = local_index.setdefault(key, len(local_index))
        return pltpu.make_async_copy(src, dst, local_sems.at[n])

    whole = {"q": k.wq, "u": k.wu, "d": k.wd}

    def main(b, w):
        return pl.ds(0, R * 2 // 3 if (b, w) in SPLIT else R)

    rest = pl.ds(R * 2 // 3, R // 3)

    def w_main(b, w, fz, qi=q):
        some = main(b, w)
        return k.wd.at[b, fz, qi, c, some] if w == "d" else whole[w].at[b, fz, c, some, cut(qi, D)]

    def w_rest(b, w, fz):
        return k.wd.at[b, fz, :, c, rest] if w == "d" else whole[w].at[b, fz, c, rest]

    def w_half(b, w, fz):
        return k.wd.at[b, fz, :, c] if w == "d" else whole[w].at[b, fz, c]

    def like_main(b, w, n, m=1):
        some = main(b, w)
        return k.wd.at[b, pl.ds(0, n), pl.ds(0, m), 0, some] if w == "d" else whole[w].at[b, pl.ds(0, n), 0, some, pl.ds(0, m * D)]

    def like_rest(b, w, n):
        return k.wd.at[b, pl.ds(0, n), :, 0, rest] if w == "d" else whole[w].at[b, pl.ds(0, n), 0, rest]

    def w_z(b, w):
        for r in (1, 3, 2) if (b, w) in DIRECT else (1, 3):
            p = w_main(b, w, f)
            send(("wz", b, w), p, p, at_z(r))
        if (b, w) in SPLIT:
            for r in (1, 3):
                p = w_rest(b, w, f)
                send(("wr", b, w), p, p, at_z(r))

    def w_to_q(b, w, some):
        for r in some:
            for j in range(1, 4):
                p = w_main(b, w, z_peer[r])
                send(("wq", b, w), p, p, at_q(j))

    def w_zq(b, w):
        if (b, w) in DIRECT:
            wait("recv", ("wz", b, w), lambda: like_main(b, w, 3))
        else:
            wait("recv", ("wm", b, w), lambda: like_main(b, w, 1))
        if (b, w) in STEPS:
            for r in (1, 3, 2):
                p = w_main(b, w, z_peer[r])
                send(("w1", b, w), p, p, at(first))
        else:
            w_to_q(b, w, (1, 3, 2))

    def w_q2(b, w):
        wait("recv", ("w1", b, w), lambda: like_main(b, w, 3))
        for qi in (q, first):
            for r in (1, 3, 2):
                p = w_main(b, w, z_peer[r], qi)
                send(("wq", b, w), p, p, at(second))

    def w_relay(b, w):
        if (b, w) not in DIRECT:
            wait("recv", ("wz", b, w), lambda: like_main(b, w, 2))
            p = w_main(b, w, z_peer[3])
            send(("wm", b, w), p, p, at_z(1))
        if (b, w) in SPLIT:
            wait("recv", ("wr", b, w), lambda: like_rest(b, w, 2))
            p = w_rest(b, w, z_peer[3])
            send(("wo", b, w), p, p, at_z(1))
        if (b, w) not in DIRECT and (b, w) not in STEPS:
            w_to_q(b, w, (1, 3))

    def w_opposite(b, w):
        wait("recv", ("wm", b, w), lambda: like_main(b, w, 1))
        w_to_q(b, w, (2,))

    def w_qc(b, w):
        if (b, w) in SPLIT:
            wait("recv", ("wo", b, w), lambda: like_rest(b, w, 1))
        wait("recv", ("wq", b, w), lambda: like_main(b, w, 3, 2 if (b, w) in STEPS else 3))
        for r in range(1, F):
            p = w_half(b, w, z_peer[r])
            send(("wc", b, w), p, p, at_c())

    def w_ready(b, w):
        wait("recv", ("wc", b, w), lambda: k.wd.at[b, pl.ds(0, F - 1), :, 0] if w == "d" else whole[w].at[b, pl.ds(0, F - 1), 0])

    def cols():
        return one_hot((D, D // F), lambda r, s: r == f * (D // F) + s)

    def cond_tile():
        v = k.cd[...].astype(f32)
        a = v / (1.0 + jnp.exp(-v))
        k.cz[f] = jnp.concatenate([a] * 4, axis=0).astype(bf)

    def cond_z():
        for r in range(1, F):
            send(("cz",), k.cz.at[f], k.cz.at[f], at_z(r))

    def cond_zq():
        pick = one_hot((16, F * 16), lambda r, s: (r // 4 == s // 16) & (r % 4 == s % 16)).astype(bf)
        k.cg[q, c] = dot(pick, k.cz[...].reshape(F * 16, D)).astype(bf)
        for j in range(1, 4):
            send(("cq",), k.cg.at[q, c], k.cg.at[q, c], at_q(j))

    def cond_qc():
        wait("recv", ("cq",), lambda: k.cg.at[pl.ds(0, 3), 0])
        send(("cc",), k.cg.at[:, c], k.cg.at[:, c], at_c())

    def cond_ready():
        wait("recv", ("cc",), lambda: k.cg.at[:, 0])

    def tile_mask(n, p):
        r = lax.broadcasted_iota(jnp.int32, (n, 1), 0)
        return jnp.where((r // 4) % 4 == p, 1.0, 0.0)

    tiles = ((0, 1), (1, 3))

    def mod_partial(part):
        a = dot(k.cz[...].reshape(F * 16, D), cols().astype(bf))
        masked = [(a * tile_mask(F * 16, p)).astype(bf) for p in range(4)]
        lo, hi = tiles[part]
        for t in range(lo, hi):
            total = None
            for p in range(4):
                b, m = divmod(4 * t + p, 6)
                o = dot(masked[p], k.wa[b, :, m * D : (m + 1) * D])
                total = o if total is None else total + o
            k.ms[:, 16 * t : 16 * t + 16, :] = total.astype(bf).reshape(F, 16, D)
        some = pl.ds(16 * lo, 16 * (hi - lo))
        for r in range(1, F):
            send(("mz", part), k.ms.at[z_peer[r], some], k.mr.at[f, some], at_z(r))

    def mod_ready(part):
        lo, hi = tiles[part]
        some = slice(16 * lo, 16 * hi)
        wait("recv", ("mz", part), lambda: k.mr.at[pl.ds(0, F - 1), pl.ds(16 * lo, 16 * (hi - lo))])
        total = k.ms[f, some].astype(f32)
        for r in range(1, F):
            total = total + k.mr[z_peer[r], some].astype(f32)
        k.mod[2 * lo : 2 * hi] = total.reshape(2 * (hi - lo), 2 * I, D)

    def piece(b, i, p):
        at = p % 2 * I + i
        return k.mod[3 * b + p // 2, at : at + 1, :]

    def dm_row(b, i, p, v):
        to, at = (k.dm, (p - 2) * I + i) if p >= 2 else (k.dl, p * I + i)
        to[b, at : at + 1, :] = v

    def dm_pieces(t):
        return [(t, p + 2) for p in range(4)] if t < B else [(p // 2, p % 2) for p in range(4)]

    def dm_start(t):
        k.dg[t, q, c, f] = (k.dm[t] if t < B else k.dl[...].reshape(4 * I, D)).astype(bf)
        for r in range(1, F):
            p = k.dg.at[t, q, c, f]
            send(("dz", t), p, p, at_z(r))

    def dm_zq(t):
        wait("recv", ("dz", t), lambda: k.dg.at[t, 0, 0, pl.ds(0, F - 1)])
        for j in range(1, 4):
            p = k.dg.at[t, q, c]
            send(("dq", t), p, p, at_q(j))

    def dm_qc(t):
        wait("recv", ("dq", t), lambda: k.dg.at[t, pl.ds(0, 3), 0])
        p = k.dg.at[t, :, c]
        send(("dc", t), p, p, at_c())

    def dm_ready(t):
        wait("recv", ("dc", t), lambda: k.dg.at[t, :, 0])

    def dcond_part(t):
        tile = k.dg[t, q, c].reshape(F * 16, D).astype(f32)
        acc = None
        for p, (b, m) in enumerate(dm_pieces(t)):
            o = dot((tile * tile_mask(F * 16, p)).astype(bf), k.wa[b, :, m * D : (m + 1) * D], NT)
            acc = o if acc is None else acc + o
        return acc

    def dcond_send():
        acc = dcond_part(0) + dcond_part(1) + dcond_part(2)
        fold = one_hot((F * 8, F * 16), lambda r, s: (r // 8 == s // 16) & (r % 8 == s % 4))
        t = exact_dot(exact_dot(fold, acc), cols(), NT)
        k.cs[...] = t.reshape(F, 8, D)
        for r in range(1, F):
            send(("gz",), k.cs.at[z_peer[r]], k.cr.at[f], at_z(r))

    def dcond_finish():
        wait("recv", ("gz",), lambda: k.cr.at[pl.ds(0, F - 1)])
        total = k.cs[f]
        for r in range(1, F):
            total = total + k.cr[z_peer[r]]
        v = k.cd[...].astype(f32)
        s = 1.0 / (1.0 + jnp.exp(-v))
        k.gc[:I] = total[:I] * (s * (1.0 + v * (1.0 - s)))
        local(("grad_cond",), k.gc.at[pl.ds(0, I)], out.grad_cond).start()

    def ada_copy(b, m):
        stage = (k.xs.at[1], k.mid.at[1])[b]
        return local(("ada", b, m), stage.at[pl.ds(m * (D // F), D // F)], out.grad_ada.at[b, :, pl.ds(m * D, D)])

    def grad_ada(t):
        n = GROUP * F * 16
        a = dot(k.cg[...].reshape(n // 4, D), cols().astype(bf)).astype(bf)
        spread = one_hot((n, n // 4), lambda r, s: (r // 16 == s // 4) & (r % 4 == s % 4)).astype(bf)
        a = dot(spread, a)
        tile = k.dg[t].reshape(n, D)
        for p, (b, m) in enumerate(dm_pieces(t)):
            stage = (k.xs.at[1], k.mid.at[1])[b]
            stage[m * (D // F) : (m + 1) * (D // F), :] = dot((a * tile_mask(n, p)).astype(bf), tile, TN)
            ada_copy(b, m).start()

    def width(w):
        return W if w[0] == "q" else D

    def g_local(w):
        return k.gq.at[int(w[1])] if w[0] == "q" else {"u": k.gu, "d": k.gd}[w]

    def g_halves(b, w):
        return k.hq.at[b, int(w[1])] if w[0] == "q" else {"u": k.hu, "d": k.hd}[w].at[b]

    def g_result(b, w):
        return k.oq.at[b, int(w[1])] if w[0] == "q" else {"u": k.ou, "d": k.od}[w].at[b]

    def g_buf(b, w, kind):
        return getattr(k, f"{kind}{w}{b}")

    def quarter(w, h, qi):
        return h.at[:, qi] if w == "d" else h.at[:, :, cut(qi, width(w))]

    def one_of(w, ref, j):
        return ref.at[q_peer[j]] if w == "d" else ref.at[:, cut(q_peer[j], width(w))]

    def r_piece(b, w):
        return k.od.at[b, q, c] if w == "d" else g_result(b, w).at[c, :, cut(q, width(w))]

    def r_half(b, w):
        return k.od.at[b, :, c] if w == "d" else g_result(b, w).at[c]

    def g_c(b, w):
        half = k.gd.at[:, :, other] if w == "d" else g_local(w).at[:, other]
        send(("gc", b, w), half, g_halves(b, w), at_c())

    def g_1(b, w):
        h = g_halves(b, w)
        for kind in ("send", "recv"):
            wait(kind, ("gc", b, w), lambda: g_halves(b, w))
        for n in range(F):
            own = k.gd[n, :, c] if w == "d" else g_local(w)[n, c]
            h[n] = h[n] + own
        how = METHOD[b][w]
        if how == "direct":
            for r, j in [(r, j) for r in range(F) for j in range(4)][1:]:
                send(("g1", b, w), h.at[z_peer[r], :, cut(q_peer[j], W)], g_buf(b, w, "a").at[r * 4 + j], at_q(j, r))
        elif how == "steps":
            for n, qi in enumerate((first, across)):
                send(("gt", b, w), quarter(w, h, qi), g_buf(b, w, "t").at[n], at(first))
        elif how == "ring":
            send(("gt", b, w), h.at[z_peer[2]], g_buf(b, w, "t"), at_z(1))
        else:
            for j in range(1, 4):
                send(("g1", b, w), quarter(w, h, q_peer[j]), g_buf(b, w, "a").at[j - 1], at_q(j))

    def g_fly(b, w):
        h, t = g_halves(b, w), g_buf(b, w, "t")
        wait("recv", ("gt", b, w), lambda: t)
        for n, qi in enumerate((q, second)):
            p = quarter(w, h, qi)
            p[...] = p[...] + t[n]
        send(("g1", b, w), quarter(w, h, second), g_buf(b, w, "a"), at(second))

    def g_ring(b, w):
        h, t = g_halves(b, w), g_buf(b, w, "t")
        wait("recv", ("gt", b, w), lambda: t)
        h[z_peer[1]] = h[z_peer[1]] + t[...]
        for n, r in enumerate((1, 3)):
            send(("g1", b, w), h.at[z_peer[r]], g_buf(b, w, "a").at[n], at_z(r))

    def g_direct(b, w):
        h, a = g_halves(b, w), g_buf(b, w, "a")
        wait("recv", ("g1", b, w), lambda: a.at[pl.ds(0, 4 * F - 1)])
        total = h[f, :, cut(q, W)].astype(f32)
        for n in range(1, 4 * F):
            total = total + a[n].astype(f32)
        hand_back(b, w, total)

    def hand_back(b, w, total):
        p = r_piece(b, w)
        p[...] = total.astype(bf)
        for j in range(1, 4):
            send(("g3", b, w), p, p, at_q(j))
        if (b, w) in ONE:
            for j in range(4):
                send(("g3", b, w), p, p, at_c(j))

    def g_2(b, w):
        h, a, s = g_halves(b, w), g_buf(b, w, "a"), g_buf(b, w, "s")
        wait("recv", ("g1", b, w), lambda: a)
        if METHOD[b][w] == "ring":
            total = h[f].astype(f32) + a[0].astype(f32) + a[1].astype(f32)
            s[...] = total.astype(bf)
            for j in range(1, 4):
                send(("g2", b, w), one_of(w, s, j), g_buf(b, w, "b").at[j - 1], at_q(j))
        else:
            if METHOD[b][w] == "steps":
                s[...] = quarter(w, h, q)[...] + a[...]
            else:
                total = quarter(w, h, q)[...].astype(f32)
                for j in range(3):
                    total = total + a[j].astype(f32)
                s[...] = total.astype(bf)
            for r in range(1, F):
                send(("g2", b, w), s.at[z_peer[r]], g_buf(b, w, "b").at[f], at_z(r))

    def g_3(b, w):
        s, a = g_buf(b, w, "s"), g_buf(b, w, "b")
        if METHOD[b][w] == "ring":
            wait("recv", ("g2", b, w), lambda: a)
            total = one_of(w, s, 0)[...].astype(f32)
            for j in range(3):
                total = total + a[j].astype(f32)
        else:
            wait("recv", ("g2", b, w), lambda: a.at[pl.ds(0, F - 1)])
            total = s[f].astype(f32)
            for r in range(1, F):
                total = total + a[z_peer[r]].astype(f32)
        hand_back(b, w, total)

    def g_4(b, w):
        wait("recv", ("g3", b, w), lambda: k.od.at[b, pl.ds(0, 3), 0] if w == "d" else g_result(b, w).at[0, :, pl.ds(0, 3 * width(w))])
        send(("g4", b, w), r_half(b, w), r_half(b, w), at_c())

    def out_copy(b, w):
        to = out.grad_q.at[b, int(w[1])] if w[0] == "q" else {"u": out.grad_u, "d": out.grad_d}[w].at[b]
        return local(("out", b, w), g_result(b, w), to)

    def seven(b, w):
        return k.act.at[pl.ds(0, 7 * R), pl.ds(0, width(w))]

    def g_5(b, w):
        if (b, w) in ONE:
            wait("recv", ("g3", b, w), lambda: seven(b, w))
        else:
            wait("recv", ("g4", b, w), lambda: k.od.at[b, :, 0] if w == "d" else g_result(b, w).at[0])
        out_copy(b, w).start()

    def m_qkv(b):
        return k.wq[b, :, :, :, : 3 * D].reshape(D, 3 * D)

    def m_proj(b):
        return k.wq[b, :, :, :, 3 * D :].reshape(D, D)

    def m_up(b, at, n):
        return k.wu[b, :, :, :, at : at + n].reshape(D, n)

    def m_down(b):
        return k.wd[b].reshape(FF, D)

    def state(b, i):
        return k.xs[b, rows(i), :]

    def lane_masks():
        lane = lax.broadcasted_iota(jnp.int32, (1, 2 * HS), 1)
        lo = jnp.where(lane < HS, 1.0, 0.0)
        return lo.astype(bf), (1.0 - lo).astype(bf)

    def head_cols(p, which):
        return slice(p * D + which * W, p * D + (which + 1) * W)

    def fwd_norm(b, i):
        hat, _ = norm_hat(state(b, i))
        k.fi[b, rows(i), :] = (hat * (1.0 + piece(b, i, 1)) + piece(b, i, 0)).astype(bf)

    def fwd_qkv(b, i):
        r = rows(i)
        y = dot(k.fi[b, r, :], m_qkv(b))
        for p in range(PAIRS):
            s = head_cols(p, 0)
            k.qkv[b, r, s] = (y[:, s] * HS**-0.5).astype(bf)
            s = slice(p * D + W, (p + 1) * D)
            k.qkv[b, r, s] = y[:, s].astype(bf)

    def fwd_probs(b, i):
        masks = lane_masks()
        for h in range(HEADS):
            qs = k.qkv[b, rows(i), head_cols(h // 2, 0)]
            ks = k.qkv[b, rows(i), head_cols(h // 2, 1)]
            scores = dot(ks * masks[h % 2], qs, NT)
            ex = jnp.exp(scores - jnp.max(scores, axis=0, keepdims=True))
            k.pt[b, i * HEADS + h] = (ex * (1.0 / jnp.sum(ex, axis=0, keepdims=True))).astype(bf)

    def fwd_mix(b, i):
        mixed = []
        for p in range(PAIRS):
            vt = k.qkv[b, rows(i), head_cols(p, 2)].T
            for m in range(2):
                mixed.append(dot(vt[m * HS : (m + 1) * HS], k.pt[b, i * HEADS + 2 * p + m]))
        k.mt[b, :, rows(i)] = jnp.concatenate(mixed, axis=0).astype(bf)

    def fwd_proj(b, i):
        r = rows(i)
        att = dot(k.mt[b, :, r], m_proj(b), TN)
        k.att[b, r, :] = att.astype(bf)
        mid = state(b, i) + piece(b, i, 2) * att
        k.mid[b, r, :] = mid
        hat, _ = norm_hat(mid)
        k.si[b, r, :] = (hat * (1.0 + piece(b, i, 4)) + piece(b, i, 3)).astype(bf)

    def fwd_up(b):
        n = FF // 3
        for j in range(3):
            s = slice(j * n, (j + 1) * n)
            x = dot(k.si[b], m_up(b, j * n, n))
            k.hid[b, :, s] = x.astype(bf)
            k.act[:, s] = (x * (0.5 * jnp.tanh(x * (GELU_A + GELU_B * (x * x))) + 0.5)).astype(bf)

    def fwd_down(b):
        acc = dot(k.act[...], m_down(b))
        k.br[b] = acc.astype(bf)
        for i in images:
            r = rows(i)
            k.xs[b + 1, r, :] = k.mid[b, r, :] + piece(b, i, 5) * acc[r]

    def turn():
        for i in images:
            r = rows(i)
            k.da[r, :] = k.xs[B, r, :].astype(bf)
            k.xs[B, r, :] = k.db[r, :].astype(f32) * inp.mask[i].astype(f32)

    def bwd_hidden(b):
        for i in images:
            r = rows(i)
            g = k.xs[B, r, :]
            dm_row(b, i, 5, jnp.sum(g * k.br[b, r, :].astype(f32), axis=0, keepdims=True))
            k.db[r, :] = (g * piece(b, i, 5)).astype(bf)
        n = FF // 2
        for h in range(2):
            r = slice(h * T // 2, (h + 1) * T // 2)
            for j in range(2):
                s = slice(j * n, (j + 1) * n)
                da = dot(k.db[r, :], m_down(b)[s], NT)
                a, slope = gelu_parts(k.hid[b, r, s].astype(f32))
                k.act[r, s] = a.astype(bf)
                k.hid[b, r, s] = (slope * da).astype(bf)

    def bwd_second(b):
        acc = dot(k.hid[b], m_up(b, 0, FF), NT)
        for i in images:
            r = rows(i)
            d = acc[r]
            hat, rs = norm_hat(k.mid[b, r, :])
            dm_row(b, i, 3, jnp.sum(d, axis=0, keepdims=True))
            dm_row(b, i, 4, jnp.sum(d * hat, axis=0, keepdims=True))
            d_mid = k.xs[B, r, :] + norm_back(d * (1.0 + piece(b, i, 4)), hat, rs)
            k.xs[B, r, :] = d_mid
            dm_row(b, i, 2, jnp.sum(d_mid * k.att[b, r, :].astype(f32), axis=0, keepdims=True))
            k.da[r, :] = (d_mid * piece(b, i, 2)).astype(bf)

    def grad_down(b):
        n = FF // 2
        for h in range(2):
            x = dot(k.act[:, h * n : (h + 1) * n], k.db[...], TN)
            k.gd[h * F // 2 : (h + 1) * F // 2] = x.astype(bf).reshape(F // 2, 4, 2, R, D)

    def grad_up(b):
        n = FF // 2
        for h in range(2):
            s = slice(h * n, (h + 1) * n)
            k.gu[:, :, :, s] = dot(k.si[b], k.hid[b, :, s], TN).astype(bf).reshape(F, 2, R, n)

    def grad_proj(b):
        x = dot(k.mt[b], k.da[...]).astype(bf).reshape(F, 2, R, D)
        for p in range(PAIRS):
            k.gq[p, :, :, :, 3 * W :] = x[:, :, :, p * W : (p + 1) * W]

    def grad_qkv(b, p):
        x = dot(k.fi[b], k.qkv[b, :, p * D : (p + 1) * D], TN)
        k.gq[p, :, :, :, : 3 * W] = x.astype(bf).reshape(F, 2, R, 3 * W)

    def bwd_heads(b, p):
        masks = lane_masks()

        def ds_at(i, m):
            return slice(i * L, (i + 1) * L), slice(m * L, (m + 1) * L)

        wp = m_proj(b)[p * W : (p + 1) * W]
        for i in images:
            r = rows(i)
            do = dot(k.da[r, :], wp, NT).astype(bf)
            k.db[r, :W] = do
            vs = k.qkv[b, r, head_cols(p, 2)]
            for m in range(2):
                dp = dot(vs * masks[m], do, NT)
                pf = k.pt[b, i * HEADS + 2 * p + m].astype(f32)
                w = pf * dp
                k.act[ds_at(i, m)] = (w - pf * jnp.sum(w, axis=0, keepdims=True)).astype(bf)
        for i in images:
            r = rows(i)
            do = k.db[r, :W]
            qs = k.qkv[b, r, head_cols(p, 0)]
            ks = k.qkv[b, r, head_cols(p, 1)]
            kt = ks.T
            ds = [k.act[ds_at(i, m)] for m in range(2)]
            pt = [k.pt[b, i * HEADS + 2 * p + m] for m in range(2)]
            dk = dot(ds[0], qs * masks[0]) + dot(ds[1], qs * masks[1])
            dv = dot(pt[0], do * masks[0]) + dot(pt[1], do * masks[1])
            dq = jnp.concatenate([dot(kt[m * HS : (m + 1) * HS], ds[m]) for m in range(2)], axis=0)
            k.qkv[b, r, head_cols(p, 1)] = dk.astype(bf)
            k.qkv[b, r, head_cols(p, 2)] = dv.astype(bf)
            k.qkv[b, r, head_cols(p, 0)] = (dq * HS**-0.5).astype(bf).T

    def bwd_first(b, some):
        for i in some:
            r = rows(i)
            d = dot(k.qkv[b, r, :], m_qkv(b), NT)
            hat, rs = norm_hat(state(b, i))
            dm_row(b, i, 0, jnp.sum(d, axis=0, keepdims=True))
            dm_row(b, i, 1, jnp.sum(d * hat, axis=0, keepdims=True))
            k.xs[B, r, :] = k.xs[B, r, :] + norm_back(d * (1.0 + piece(b, i, 1)), hat, rs)

    def run(*todo):
        for fn, *args in todo:
            fn(*args)

    def each(fn, b):
        for i in images:
            fn(b, i)

    def out_wait():
        local(("os",), k.da, out.output).wait()

    def at_block(b, which, *todo):
        pl.when(b == which)(functools.partial(run, *todo))

    def phase(*todo):
        pl.when(me >= 0)(functools.partial(run, *todo))

    barrier = pltpu.get_barrier_semaphore()
    everyone = [at_q(j, r) for r in range(F) for j in range(4)][1:] + [at_c(j) for j in range(4)]
    for peer in everyone:
        pl.semaphore_signal(barrier, inc=1, device_id=peer, device_id_type=MESH)
    cond_load = local(("cd",), inp.cond, k.cd)
    cond_load.start()
    ada_load = local(("wa",), inp.ada, k.wa)
    w_loads = {"q": [], "u": [local(("wu",), inp.up_w, k.wu.at[:, f])], "d": [local(("wd",), inp.down_w, k.wd.at[:, f])]}
    for which in range(3):
        for p in range(PAIRS):
            w_loads["q"].append(
                local(
                    ("wq", which, p),
                    inp.qkv_w.at[:, :, :, pl.ds(which * D + p * W, W)],
                    k.wq.at[:, f, :, :, pl.ds(p * D + which * W, W)],
                )
            )
    w_loads["q"].append(local(("wp",), inp.proj_w, k.wq.at[:, f, :, :, pl.ds(3 * D, D)]))
    other_loads = [local(("tk",), inp.tokens, k.da), local(("db",), inp.cotangent, k.db)]
    for copy in w_loads["q"] + [ada_load] + w_loads["u"] + w_loads["d"] + other_loads:
        copy.start()
    cond_load.wait()
    cond_tile()
    for copy in w_loads["q"] + [ada_load] + w_loads["u"] + w_loads["d"] + other_loads:
        copy.wait()
    for i in images:
        k.xs[0, rows(i), :] = k.da[rows(i), :].astype(f32)
    pl.semaphore_wait(barrier, len(everyone))

    run((cond_z,), (w_z, 1, "q"), (w_z, 0, "q"), (wait, "recv", ("cz",), k.cz.at[pl.ds(0, F - 1)]), (w_z, 0, "u"), (mod_partial, 0), (w_z, 0, "d"), (w_relay, 1, "q"), (cond_zq,), (w_zq, 0, "q"), (w_zq, 0, "u"), (w_z, 1, "u"), (mod_ready, 0))

    def forward(step, _):
        b = step
        phase((each, fwd_norm, b),)
        at_block(b, 0, (w_zq, 0, "d"), (w_relay, 0, "d"), (w_qc, 0, "q"), (mod_partial, 1), (w_opposite, 1, "q"), (w_ready, 0, "q"))
        phase((each, fwd_qkv, b),)
        at_block(b, 0, (w_relay, 1, "u"), (w_z, 1, "d"))
        phase((each, fwd_probs, b), (each, fwd_mix, b))
        at_block(b, 0, (w_qc, 0, "u"), (mod_ready, 1))
        at_block(b, 1, (w_qc, 1, "u"),)
        phase((each, fwd_proj, b),)
        at_block(b, 0, (w_ready, 0, "u"), (w_qc, 0, "d"), (w_opposite, 1, "u"))
        at_block(b, 1, (w_qc, 1, "d"), (w_ready, 1, "u"))
        phase((fwd_up, b),)
        at_block(b, 0, (w_qc, 1, "q"), (w_ready, 0, "d"))
        at_block(b, 1, (w_ready, 1, "d"),)
        phase((fwd_down, b),)
        at_block(b, 0, (w_zq, 1, "d"), (w_relay, 1, "d"), (w_ready, 1, "q"))
        return 0

    lax.fori_loop(0, B, forward, 0)
    phase((turn,),)
    out_load = local(("os",), k.da, out.output)
    out_load.start()

    def backward(step, _):
        b = B - 1 - step
        phase((bwd_hidden, b),)
        at_block(b, 0, (dm_zq, 1), (g_fly, 1, "q0"), (g_2, 1, "d"))
        phase((grad_up, b),)
        at_block(b, 1, (g_c, 1, "u"),)
        at_block(b, 0, (g_c, 0, "u"), (g_3, 1, "u"))
        phase((grad_down, b),)
        at_block(b, 1, (g_c, 1, "d"), (g_1, 1, "u"))
        at_block(b, 0, (g_c, 0, "d"), (g_fly, 1, "q1"), (g_1, 0, "u"), (g_2, 1, "q0"))
        at_block(b, B - 1, (out_wait,))
        phase((bwd_second, b),)
        at_block(b, 1, (g_1, 1, "d"), (dm_start, 1))
        at_block(b, 0, (g_1, 0, "d"), (dm_start, 0), (g_4, 1, "u"), (g_2, 1, "q1"))
        phase((grad_proj, b),)
        phase((bwd_heads, b, 0),)
        at_block(b, 0, (g_5, 1, "u"), (g_3, 1, "q0"))
        phase((grad_qkv, b, 0),)
        at_block(b, 1, (g_c, 1, "q0"),)
        at_block(b, 0, (g_c, 0, "q0"),)
        phase((bwd_heads, b, 1),)
        at_block(b, 1, (g_1, 1, "q0"),)
        at_block(b, 0, (g_3, 1, "d"), (g_1, 0, "q0"))
        phase((grad_qkv, b, 1),)
        at_block(b, 1, (g_c, 1, "q1"),)
        at_block(b, 0, (g_c, 0, "q1"), (g_3, 1, "q1"), (g_2, 0, "u"))
        phase((bwd_heads, b, 2),)
        at_block(b, 1, (g_1, 1, "q1"), (g_2, 1, "u"))
        at_block(b, 0, (g_1, 0, "q1"),)
        phase((grad_qkv, b, 2),)
        at_block(b, 1, (g_c, 1, "q2"),)
        at_block(b, 0, (g_c, 0, "q2"), (g_fly, 0, "d"), (g_ring, 0, "q0"))
        phase((bwd_first, b, images[: I // 2]),)
        at_block(b, 0, (g_1, 0, "q2"),)
        phase((bwd_first, b, images[I // 2 :]),)
        at_block(b, 1, (g_1, 1, "q2"),)
        return 0

    lax.fori_loop(0, B, backward, 0)
    run((dm_start, 2),)
    g_load = local(("g",), k.xs.at[B], out.grad_tokens)
    g_load.start()
    run((g_4, 1, "d"), (g_2, 1, "q2"), (g_fly, 0, "q1"), (cond_qc,), (dm_qc, 1), (dm_zq, 0), (g_4, 1, "q0"), (g_4, 1, "q1"), (g_3, 0, "u"), (g_5, 1, "d"), (g_2, 0, "d"), (cond_ready,), (dm_ready, 1), (grad_ada, 1), (g_5, 1, "q1"), (g_5, 1, "q0"), (g_2, 0, "q0"), (g_2, 0, "q2"), (g_2, 0, "q1"), (dm_zq, 2), (dcond_send,), (g_3, 1, "q2"), (dm_qc, 0), (dm_ready, 0), (grad_ada, 0), (g_4, 0, "u"), (g_3, 0, "q0"), (g_3, 0, "d"), (g_5, 0, "u"), (g_3, 0, "q2"), (dm_qc, 2), (g_3, 0, "q1"), (g_4, 1, "q2"), (dcond_finish,), (dm_ready, 2), (grad_ada, 2), (g_4, 0, "q0"), (g_5, 1, "q2"), (g_4, 0, "d"), (g_5, 0, "q0"), (g_4, 0, "q2"), (g_5, 0, "d"), (all_sent,), (g_5, 0, "q1"), (g_5, 0, "q2"), (all_sent,))
    g_load.wait()
    local(("grad_cond",), k.gc.at[pl.ds(0, I)], out.grad_cond).wait()
    for b in range(B):
        for m in range(6):
            ada_copy(b, m).wait()
        for w in KINDS:
            out_copy(b, w).wait()
    assert len(index) <= N_SEMS and len(local_index) <= N_LOCAL


def finish(*refs):
    n = len(OUTPUTS)
    src, dst, low, high, mid, sems = refs[:n], refs[n : 2 * n + 1], refs[2 * n + 1 : 2 * n + 4], refs[2 * n + 4 : -5], refs[-5:-1], refs[-1]
    B, pairs, _, R, four = src[4].shape
    W = four // 4
    D = W * pairs
    copies = []

    def copy(a, b):
        copies.append(pltpu.make_async_copy(a, b, sems.at[len(copies)]))
        copies[-1].start()
        return copies[-1]

    loads = [copy(src[4 + m], low[m]) for m in range(3)]
    through = [copy(src[m], mid[m]) for m in range(4)]
    qkv, proj, up, down = high
    loads[0].wait()
    for b in range(B):
        for p in range(pairs):
            x = low[0][b, p].reshape(2 * R, 4 * W).astype(f32)
            for j in range(3):
                qkv[b, :, j * D + p * W : j * D + (p + 1) * W] = x[:, j * W : (j + 1) * W]
            proj[b, :, p * W : (p + 1) * W] = x[:, 3 * W :]
    copy(qkv, dst[4])
    copy(proj, dst[5])
    loads[1].wait()
    up[...] = low[1][...].reshape(up.shape).astype(f32)
    copy(up, dst[6])
    loads[2].wait()
    down[...] = low[2][...].reshape(down.shape).astype(f32)
    copy(down, dst[7])
    for m in range(4):
        through[m].wait()
        copy(mid[m], dst[m])
    for c in copies[7:]:
        c.wait()


def body(F, tokens, cond, cotangent, keep_mask, w_ada, w_qkv, w_proj, w_up, w_down):
    I, L, D = tokens.shape
    B, _, FF = w_up.shape
    R = D // F // 2
    W = D // PAIRS
    T = I * L
    shapes = scratch(F, I, L, D, FF, B)
    names = tuple(shapes)
    anywhere = pl.BlockSpec(memory_space=pl.ANY)
    results = [
        jax.ShapeDtypeStruct((T, D), bf),
        jax.ShapeDtypeStruct((T, D), f32),
        jax.ShapeDtypeStruct((I, D), f32),
        jax.ShapeDtypeStruct((B, D // F, 6 * D), f32),
        jax.ShapeDtypeStruct((B, PAIRS, 2, R, 4 * W), bf),
        jax.ShapeDtypeStruct((B, 2, R, FF), bf),
        jax.ShapeDtypeStruct((B, 4, 2, R, D), bf),
    ]
    found = pl.pallas_call(
        functools.partial(kernel, names, F, I, L, D, FF, B),
        name="blocks",
        out_shape=results,
        in_specs=[pl.BlockSpec(memory_space=pltpu.SMEM) if n == "mask" else anywhere for n in INPUTS],
        out_specs=[anywhere] * len(OUTPUTS),
        scratch_shapes=[pltpu.VMEM(*shapes[n]) for n in names]
        + [pltpu.SemaphoreType.DMA((N_SEMS,)), pltpu.SemaphoreType.DMA((N_LOCAL,))],
        compiler_params=pltpu.CompilerParams(
            collective_id=0, has_side_effects=True, vmem_limit_bytes=64 * 2**20 - 2**17
        ),
    )(
        tokens.reshape(T, D),
        cond,
        cotangent.reshape(T, D),
        keep_mask,
        w_ada,
        w_qkv.reshape(B, 2, R, 3 * D),
        w_proj.reshape(B, 2, R, D),
        w_up.reshape(B, 2, R, FF),
        w_down.reshape(B, 4, 2, R, D),
    )
    grads = [(B, 2 * R, 3 * D), (B, 2 * R, D), (B, 2 * R, FF), (B, 8 * R, D)]
    output, grad_tokens, grad_cond, *weights = pl.pallas_call(
        finish,
        name="finish",
        out_shape=results[:4] + [jax.ShapeDtypeStruct(s, f32) for s in grads],
        in_specs=[anywhere] * len(OUTPUTS),
        out_specs=[anywhere] * 8,
        scratch_shapes=[pltpu.VMEM(r.shape, bf) for r in results[4:]]
        + [pltpu.VMEM(s, f32) for s in grads]
        + [pltpu.VMEM(r.shape, r.dtype) for r in results[:4]]
        + [pltpu.SemaphoreType.DMA((16,))],
        compiler_params=pltpu.CompilerParams(vmem_limit_bytes=64 * 2**20 - 2**17),
    )(*found)
    if lax.axis_size("dp") > GROUP:
        first = lax.axis_index("dp") % GROUP == 0
        weights = lax.psum(tuple(jnp.where(first, w, 0.0) for w in weights), "dp")
    return (output.reshape(I, L, D), grad_tokens.reshape(I, L, D), grad_cond, *weights)


def solution(mesh):
    slots = P(("dp", "fsdp"), None, None)
    weight = P(None, "fsdp", None)
    return jax.shard_map(
        functools.partial(body, mesh.shape["fsdp"]),
        mesh=mesh,
        in_specs=(slots, P(("dp", "fsdp"), None), slots, P(("dp", "fsdp"))) + (weight,) * 5,
        out_specs=(slots, slots, P(("dp", "fsdp"), None)) + (weight,) * 5,
        check_vma=False,
    )
```

profile of v0, /device:TPU:0, one launch (start us, length us, event | category | flops | bytes accessed | tf_op | source)
XLA Modules:
  0.0 121.4 jit_solution(13499033820696458404)
XLA Ops:
  0.6 114.9 %blocks.1 = (bf16[1024,384]{1,0:T(8,128)(2,1)}, f32[1024,384]{1,0:T(8,128)}, f32[4,384]{1,0:T(4,128)}, f32[2,96,2304]{2,1,0:T(8,128)}, bf16[2,3,2,48,512]{4,3,2,...) custom-call(bf16[1024,384]{1,0:T(8,128)(2,1)} %bitcast.8, ...), custom_call_target="tpu_custom_call" | custom-call | tf_op jit(solution)/shard_map/blocks/pallas_call | solution.py:924
  115.5 5.7 %finish.1 = (bf16[1024,384]{1,0:T(8,128)(2,1)}, f32[1024,384]{1,0:T(8,128)}, f32[4,384]{1,0:T(4,128)}, f32[2,96,2304]{2,1,0:T(8,128)}, f32[2,96,1152]{2,1,0:T(8,...) custom-call(bf16[1024,384]{1,0:T(8,128)(2,1)} %get-tuple-element.23.refs_0_, ...), custom_call_target="tpu_custom_call" | custom-call | tf_op jit(solution)/shard_map/finish/pallas_call | solution.py:947
where the time goes:
time: 122 us; the launch traced here: 121 us
  Pallas kernels  121 us (99%)
    pallas_call x1, Pallas kernels, body(): pl.pallas_call(functools.partial(kernel, names, F, I, L, D, FF, B), name=...  115 us
    pallas_call x1, Pallas kernels, body(): pl.pallas_call(finish, name='finish', out_shape=results[:4] + [jax.ShapeD...  5.69 us

commit v1 on v0

--- a/solution.py
+++ b/solution.py
@@ -76,12 +76,12 @@
         xs=((B + 1, T, D), f32),
         fi=((B, T, D), bf),
         qkv=((B, T, 3 * D), bf),
-        pt=((B, I * HEADS, L, L), bf),
+        pt=((I * HEADS, L, L), bf),
         mt=((B, D, T), bf),
         att=((B, T, D), bf),
         mid=((B, T, D), f32),
         si=((B, T, D), bf),
-        hid=((B, T, FF), bf),
+        hid=((T, FF), bf),
         br=((B, T, D), bf),
         db=((T, D), bf),
         act=((T, FF), bf),
@@ -133,16 +133,17 @@
 
 INPUTS = ("tokens", "cond", "cotangent", "mask", "ada", "qkv_w", "proj_w", "up_w", "down_w")
 OUTPUTS = ("output", "grad_tokens", "grad_cond", "grad_ada", "grad_q", "grad_u", "grad_d")
+KEPT = ("pt", "hid", "act")
 N_SEMS = 256
 N_LOCAL = 64
 
 
 def kernel(names, F, I, L, D, FF, B, *refs):
-    n_in, n_out = len(INPUTS), len(OUTPUTS)
+    n_in, n_out = len(INPUTS), len(OUTPUTS) + len(KEPT)
     inp, out, k = Refs(), Refs(), Refs()
     for name, ref in zip(INPUTS, refs[:n_in]):
         setattr(inp, name, ref)
-    for name, ref in zip(OUTPUTS, refs[n_in : n_in + n_out]):
+    for name, ref in zip(OUTPUTS + KEPT, refs[n_in : n_in + n_out]):
         setattr(out, name, ref)
     for name, ref in zip(names, refs[n_in + n_out :]):
         setattr(k, name, ref)
@@ -604,19 +605,21 @@
 
     def fwd_probs(b, i):
         masks = lane_masks()
-        for h in range(HEADS):
-            qs = k.qkv[b, rows(i), head_cols(h // 2, 0)]
-            ks = k.qkv[b, rows(i), head_cols(h // 2, 1)]
-            scores = dot(ks * masks[h % 2], qs, NT)
-            ex = jnp.exp(scores - jnp.max(scores, axis=0, keepdims=True))
-            k.pt[b, i * HEADS + h] = (ex * (1.0 / jnp.sum(ex, axis=0, keepdims=True))).astype(bf)
+        for p in range(PAIRS):
+            qs = k.qkv[b, rows(i), head_cols(p, 0)]
+            ks = k.qkv[b, rows(i), head_cols(p, 1)]
+            both = dot(jnp.concatenate([ks * m for m in masks], axis=0), qs, NT)
+            for m in range(2):
+                scores = both[m * L : (m + 1) * L]
+                ex = jnp.exp(scores - jnp.max(scores, axis=0, keepdims=True))
+                k.pt[i * HEADS + 2 * p + m] = (ex * (1.0 / jnp.sum(ex, axis=0, keepdims=True))).astype(bf)
 
     def fwd_mix(b, i):
         mixed = []
         for p in range(PAIRS):
             vt = k.qkv[b, rows(i), head_cols(p, 2)].T
             for m in range(2):
-                mixed.append(dot(vt[m * HS : (m + 1) * HS], k.pt[b, i * HEADS + 2 * p + m]))
+                mixed.append(dot(vt[m * HS : (m + 1) * HS], k.pt[i * HEADS + 2 * p + m]))
         k.mt[b, :, rows(i)] = jnp.concatenate(mixed, axis=0).astype(bf)
 
     def fwd_proj(b, i):
@@ -633,8 +636,9 @@
         for j in range(3):
             s = slice(j * n, (j + 1) * n)
             x = dot(k.si[b], m_up(b, j * n, n))
-            k.hid[b, :, s] = x.astype(bf)
-            k.act[:, s] = (x * (0.5 * jnp.tanh(x * (GELU_A + GELU_B * (x * x))) + 0.5)).astype(bf)
+            a, slope = gelu_parts(x)
+            k.act[:, s] = a.astype(bf)
+            k.hid[:, s] = slope.astype(bf)
 
     def fwd_down(b):
         acc = dot(k.act[...], m_down(b))
@@ -661,12 +665,10 @@
             for j in range(2):
                 s = slice(j * n, (j + 1) * n)
                 da = dot(k.db[r, :], m_down(b)[s], NT)
-                a, slope = gelu_parts(k.hid[b, r, s].astype(f32))
-                k.act[r, s] = a.astype(bf)
-                k.hid[b, r, s] = (slope * da).astype(bf)
+                k.hid[r, s] = (k.hid[r, s].astype(f32) * da).astype(bf)
 
     def bwd_second(b):
-        acc = dot(k.hid[b], m_up(b, 0, FF), NT)
+        acc = dot(k.hid[...], m_up(b, 0, FF), NT)
         for i in images:
             r = rows(i)
             d = acc[r]
@@ -688,7 +690,7 @@
         n = FF // 2
         for h in range(2):
             s = slice(h * n, (h + 1) * n)
-            k.gu[:, :, :, s] = dot(k.si[b], k.hid[b, :, s], TN).astype(bf).reshape(F, 2, R, n)
+            k.gu[:, :, :, s] = dot(k.si[b], k.hid[:, s], TN).astype(bf).reshape(F, 2, R, n)
 
     def grad_proj(b):
         x = dot(k.mt[b], k.da[...]).astype(bf).reshape(F, 2, R, D)
@@ -711,9 +713,10 @@
             do = dot(k.da[r, :], wp, NT).astype(bf)
             k.db[r, :W] = do
             vs = k.qkv[b, r, head_cols(p, 2)]
+            both = dot(jnp.concatenate([vs * m for m in masks], axis=0), do, NT)
             for m in range(2):
-                dp = dot(vs * masks[m], do, NT)
-                pf = k.pt[b, i * HEADS + 2 * p + m].astype(f32)
+                dp = both[m * L : (m + 1) * L]
+                pf = k.pt[i * HEADS + 2 * p + m].astype(f32)
                 w = pf * dp
                 k.act[ds_at(i, m)] = (w - pf * jnp.sum(w, axis=0, keepdims=True)).astype(bf)
         for i in images:
@@ -723,7 +726,7 @@
             ks = k.qkv[b, r, head_cols(p, 1)]
             kt = ks.T
             ds = [k.act[ds_at(i, m)] for m in range(2)]
-            pt = [k.pt[b, i * HEADS + 2 * p + m] for m in range(2)]
+            pt = [k.pt[i * HEADS + 2 * p + m] for m in range(2)]
             dk = dot(ds[0], qs * masks[0]) + dot(ds[1], qs * masks[1])
             dv = dot(pt[0], do * masks[0]) + dot(pt[1], do * masks[1])
             dq = jnp.concatenate([dot(kt[m * HS : (m + 1) * HS], ds[m]) for m in range(2)], axis=0)
@@ -747,6 +750,24 @@
     def each(fn, b):
         for i in images:
             fn(b, i)
+
+    def keep(name):
+        return local(("keep", name), getattr(k, name), getattr(out, name))
+
+    def fetch(name):
+        return local(("fetch", name), getattr(out, name), getattr(k, name))
+
+    def keep_start(name):
+        keep(name).start()
+
+    def keep_wait(name):
+        keep(name).wait()
+
+    def fetch_start(name):
+        fetch(name).start()
+
+    def fetch_wait(name):
+        fetch(name).wait()
 
     def out_wait():
         local(("os",), k.da, out.output).wait()
@@ -794,17 +815,21 @@
         at_block(b, 0, (w_zq, 0, "d"), (w_relay, 0, "d"), (w_qc, 0, "q"), (mod_partial, 1), (w_opposite, 1, "q"), (w_ready, 0, "q"))
         phase((each, fwd_qkv, b),)
         at_block(b, 0, (w_relay, 1, "u"), (w_z, 1, "d"))
+        at_block(b, 1, (w_qc, 1, "u"),)
+        at_block(b, 1, (keep_wait, "pt"),)
         phase((each, fwd_probs, b), (each, fwd_mix, b))
+        at_block(b, 0, (keep_start, "pt"))
         at_block(b, 0, (w_qc, 0, "u"), (mod_ready, 1))
-        at_block(b, 1, (w_qc, 1, "u"),)
         phase((each, fwd_proj, b),)
         at_block(b, 0, (w_ready, 0, "u"), (w_qc, 0, "d"), (w_opposite, 1, "u"))
-        at_block(b, 1, (w_qc, 1, "d"), (w_ready, 1, "u"))
+        at_block(b, 1, (w_ready, 1, "u"),)
+        at_block(b, 1, (keep_wait, "hid"), (keep_wait, "act"))
         phase((fwd_up, b),)
-        at_block(b, 0, (w_qc, 1, "q"), (w_ready, 0, "d"))
-        at_block(b, 1, (w_ready, 1, "d"),)
+        at_block(b, 0, (keep_start, "hid"), (keep_start, "act"))
+        at_block(b, 0, (w_qc, 1, "q"), (w_ready, 0, "d"), (w_zq, 1, "d"))
+        at_block(b, 1, (w_qc, 1, "d"), (w_ready, 1, "d"))
         phase((fwd_down, b),)
-        at_block(b, 0, (w_zq, 1, "d"), (w_relay, 1, "d"), (w_ready, 1, "q"))
+        at_block(b, 0, (w_relay, 1, "d"), (w_ready, 1, "q"))
         return 0
 
     lax.fori_loop(0, B, forward, 0)
@@ -814,38 +839,43 @@
 
     def backward(step, _):
         b = B - 1 - step
+        at_block(b, 0, (fetch_wait, "hid"))
         phase((bwd_hidden, b),)
-        at_block(b, 0, (dm_zq, 1), (g_fly, 1, "q0"), (g_2, 1, "d"))
+        at_block(b, 0, (dm_zq, 1),)
         phase((grad_up, b),)
         at_block(b, 1, (g_c, 1, "u"),)
-        at_block(b, 0, (g_c, 0, "u"), (g_3, 1, "u"))
+        at_block(b, 0, (g_c, 0, "u"), (g_fly, 1, "q0"), (g_3, 1, "u"), (g_2, 1, "d"))
+        at_block(b, 0, (fetch_wait, "act"))
         phase((grad_down, b),)
         at_block(b, 1, (g_c, 1, "d"), (g_1, 1, "u"))
-        at_block(b, 0, (g_c, 0, "d"), (g_fly, 1, "q1"), (g_1, 0, "u"), (g_2, 1, "q0"))
+        at_block(b, 0, (g_c, 0, "d"), (g_1, 0, "u"), (g_fly, 1, "q1"))
         at_block(b, B - 1, (out_wait,))
         phase((bwd_second, b),)
+        at_block(b, 1, (fetch_start, "hid"))
         at_block(b, 1, (g_1, 1, "d"), (dm_start, 1))
-        at_block(b, 0, (g_1, 0, "d"), (dm_start, 0), (g_4, 1, "u"), (g_2, 1, "q1"))
+        at_block(b, 0, (g_1, 0, "d"), (dm_start, 0), (g_2, 1, "q0"))
         phase((grad_proj, b),)
+        at_block(b, 0, (fetch_wait, "pt"))
         phase((bwd_heads, b, 0),)
-        at_block(b, 0, (g_5, 1, "u"), (g_3, 1, "q0"))
+        at_block(b, 0, (g_4, 1, "u"),)
         phase((grad_qkv, b, 0),)
         at_block(b, 1, (g_c, 1, "q0"),)
         at_block(b, 0, (g_c, 0, "q0"),)
         phase((bwd_heads, b, 1),)
         at_block(b, 1, (g_1, 1, "q0"),)
-        at_block(b, 0, (g_3, 1, "d"), (g_1, 0, "q0"))
+        at_block(b, 0, (g_1, 0, "q0"), (g_5, 1, "u"))
         phase((grad_qkv, b, 1),)
         at_block(b, 1, (g_c, 1, "q1"),)
-        at_block(b, 0, (g_c, 0, "q1"), (g_3, 1, "q1"), (g_2, 0, "u"))
+        at_block(b, 0, (g_c, 0, "q1"),)
         phase((bwd_heads, b, 2),)
+        at_block(b, 1, (fetch_start, "pt"), (fetch_start, "act"))
         at_block(b, 1, (g_1, 1, "q1"), (g_2, 1, "u"))
-        at_block(b, 0, (g_1, 0, "q1"),)
+        at_block(b, 0, (g_1, 0, "q1"), (g_3, 1, "d"), (g_2, 0, "u"), (g_3, 1, "q0"), (g_2, 1, "q1"))
         phase((grad_qkv, b, 2),)
         at_block(b, 1, (g_c, 1, "q2"),)
-        at_block(b, 0, (g_c, 0, "q2"), (g_fly, 0, "d"), (g_ring, 0, "q0"))
+        at_block(b, 0, (g_c, 0, "q2"),)
         phase((bwd_first, b, images[: I // 2]),)
-        at_block(b, 0, (g_1, 0, "q2"),)
+        at_block(b, 0, (g_fly, 0, "d"), (g_ring, 0, "q0"), (g_1, 0, "q2"))
         phase((bwd_first, b, images[I // 2 :]),)
         at_block(b, 1, (g_1, 1, "q2"),)
         return 0
@@ -854,7 +884,7 @@
     run((dm_start, 2),)
     g_load = local(("g",), k.xs.at[B], out.grad_tokens)
     g_load.start()
-    run((g_4, 1, "d"), (g_2, 1, "q2"), (g_fly, 0, "q1"), (cond_qc,), (dm_qc, 1), (dm_zq, 0), (g_4, 1, "q0"), (g_4, 1, "q1"), (g_3, 0, "u"), (g_5, 1, "d"), (g_2, 0, "d"), (cond_ready,), (dm_ready, 1), (grad_ada, 1), (g_5, 1, "q1"), (g_5, 1, "q0"), (g_2, 0, "q0"), (g_2, 0, "q2"), (g_2, 0, "q1"), (dm_zq, 2), (dcond_send,), (g_3, 1, "q2"), (dm_qc, 0), (dm_ready, 0), (grad_ada, 0), (g_4, 0, "u"), (g_3, 0, "q0"), (g_3, 0, "d"), (g_5, 0, "u"), (g_3, 0, "q2"), (dm_qc, 2), (g_3, 0, "q1"), (g_4, 1, "q2"), (dcond_finish,), (dm_ready, 2), (grad_ada, 2), (g_4, 0, "q0"), (g_5, 1, "q2"), (g_4, 0, "d"), (g_5, 0, "q0"), (g_4, 0, "q2"), (g_5, 0, "d"), (all_sent,), (g_5, 0, "q1"), (g_5, 0, "q2"), (all_sent,))
+    run((g_fly, 0, "q1"), (cond_qc,), (g_2, 1, "q2"), (dm_qc, 1), (dm_zq, 0), (g_4, 1, "d"), (g_4, 1, "q0"), (cond_ready,), (dm_ready, 1), (grad_ada, 1), (g_5, 1, "d"), (g_5, 1, "q0"), (g_2, 0, "d"), (g_3, 0, "u"), (g_3, 1, "q1"), (g_2, 0, "q2"), (g_2, 0, "q1"), (g_2, 0, "q0"), (dm_zq, 2), (dcond_send,), (dm_qc, 0), (g_3, 1, "q2"), (g_4, 0, "u"), (dm_ready, 0), (grad_ada, 0), (g_4, 1, "q1"), (g_3, 0, "q0"), (g_5, 0, "u"), (g_3, 0, "d"), (g_5, 1, "q1"), (g_3, 0, "q2"), (dm_qc, 2), (g_4, 1, "q2"), (g_3, 0, "q1"), (dm_ready, 2), (grad_ada, 2), (g_4, 0, "q0"), (g_5, 1, "q2"), (dcond_finish,), (g_5, 0, "q0"), (g_4, 0, "d"), (g_4, 0, "q2"), (g_5, 0, "d"), (all_sent,), (g_5, 0, "q1"), (g_5, 0, "q2"), (all_sent,))
     g_load.wait()
     local(("grad_cond",), k.gc.at[pl.ds(0, I)], out.grad_cond).wait()
     for b in range(B):
@@ -867,7 +897,7 @@
 
 def finish(*refs):
     n = len(OUTPUTS)
-    src, dst, low, high, mid, sems = refs[:n], refs[n : 2 * n + 1], refs[2 * n + 1 : 2 * n + 4], refs[2 * n + 4 : -5], refs[-5:-1], refs[-1]
+    src, dst, high, sems = refs[:n], refs[n : 2 * n + 1], refs[2 * n + 1 : -1], refs[-1]
     B, pairs, _, R, four = src[4].shape
     W = four // 4
     D = W * pairs
@@ -876,30 +906,23 @@
     def copy(a, b):
         copies.append(pltpu.make_async_copy(a, b, sems.at[len(copies)]))
         copies[-1].start()
-        return copies[-1]
-
-    loads = [copy(src[4 + m], low[m]) for m in range(3)]
-    through = [copy(src[m], mid[m]) for m in range(4)]
+
+    for m in range(4):
+        copy(src[m], dst[m])
     qkv, proj, up, down = high
-    loads[0].wait()
     for b in range(B):
         for p in range(pairs):
-            x = low[0][b, p].reshape(2 * R, 4 * W).astype(f32)
+            x = src[4][b, p].reshape(2 * R, 4 * W).astype(f32)
             for j in range(3):
                 qkv[b, :, j * D + p * W : j * D + (p + 1) * W] = x[:, j * W : (j + 1) * W]
             proj[b, :, p * W : (p + 1) * W] = x[:, 3 * W :]
     copy(qkv, dst[4])
     copy(proj, dst[5])
-    loads[1].wait()
-    up[...] = low[1][...].reshape(up.shape).astype(f32)
+    up[...] = src[5][...].reshape(up.shape).astype(f32)
     copy(up, dst[6])
-    loads[2].wait()
-    down[...] = low[2][...].reshape(down.shape).astype(f32)
+    down[...] = src[6][...].reshape(down.shape).astype(f32)
     copy(down, dst[7])
-    for m in range(4):
-        through[m].wait()
-        copy(mid[m], dst[m])
-    for c in copies[7:]:
+    for c in copies:
         c.wait()
 
 
@@ -924,13 +947,13 @@
     found = pl.pallas_call(
         functools.partial(kernel, names, F, I, L, D, FF, B),
         name="blocks",
-        out_shape=results,
+        out_shape=[pltpu.VMEM(r.shape, r.dtype) for r in results] + [jax.ShapeDtypeStruct(*shapes[n]) for n in KEPT],
         in_specs=[pl.BlockSpec(memory_space=pltpu.SMEM) if n == "mask" else anywhere for n in INPUTS],
-        out_specs=[anywhere] * len(OUTPUTS),
+        out_specs=[anywhere] * len(OUTPUTS) + [pl.BlockSpec(memory_space=pltpu.HBM)] * len(KEPT),
         scratch_shapes=[pltpu.VMEM(*shapes[n]) for n in names]
         + [pltpu.SemaphoreType.DMA((N_SEMS,)), pltpu.SemaphoreType.DMA((N_LOCAL,))],
         compiler_params=pltpu.CompilerParams(
-            collective_id=0, has_side_effects=True, vmem_limit_bytes=64 * 2**20 - 2**17
+            collective_id=0, has_side_effects=True, vmem_limit_bytes=56 * 2**20 + 2**19
         ),
     )(
         tokens.reshape(T, D),
@@ -948,14 +971,11 @@
         finish,
         name="finish",
         out_shape=results[:4] + [jax.ShapeDtypeStruct(s, f32) for s in grads],
-        in_specs=[anywhere] * len(OUTPUTS),
+        in_specs=[pl.BlockSpec(memory_space=pltpu.VMEM)] * len(OUTPUTS),
         out_specs=[anywhere] * 8,
-        scratch_shapes=[pltpu.VMEM(r.shape, bf) for r in results[4:]]
-        + [pltpu.VMEM(s, f32) for s in grads]
-        + [pltpu.VMEM(r.shape, r.dtype) for r in results[:4]]
-        + [pltpu.SemaphoreType.DMA((16,))],
-        compiler_params=pltpu.CompilerParams(vmem_limit_bytes=64 * 2**20 - 2**17),
-    )(*found)
+        scratch_shapes=[pltpu.VMEM(s, f32) for s in grads] + [pltpu.SemaphoreType.DMA((8,))],
+        compiler_params=pltpu.CompilerParams(vmem_limit_bytes=40 * 2**20),
+    )(*found[: len(OUTPUTS)])
     if lax.axis_size("dp") > GROUP:
         first = lax.axis_index("dp") % GROUP == 0
         weights = lax.psum(tuple(jnp.where(first, w, 0.0) for w in weights), "dp")

time: 122 us -> 118 us (0.967)
  Pallas kernels: 121 us -> 117 us
    pallas_call x1, Pallas kernels: 5.69 us -> 3.18 us  [body(): pl.pallas_call(finish, name='finish', out_shape=results[:4] + [jax.ShapeD...]
    pallas_call x1, Pallas kernels: 115 us -> 114 us  [body(): pl.pallas_call(functools.partial(kernel, names, F, I, L, D, FF, B), name=...]
where the time goes in v1:
time: 118 us
  Pallas kernels  117 us (99%)
    pallas_call x1, Pallas kernels, body(): pl.pallas_call(functools.partial(kernel, names, F, I, L, D, FF, B), name=...  114 us
    pallas_call x1, Pallas kernels, body(): pl.pallas_call(finish, name='finish', out_shape=results[:4] + [jax.ShapeD...  3.18 us

profile of v1, /device:TPU:0, one launch (start us, length us, event | category | flops | bytes accessed | tf_op | source)
XLA Modules:
  0.0 117.5 jit_solution(9450876758456072389)
XLA Ops:
  0.6 113.5 %blocks.1 = (bf16[1024,384]{1,0:T(8,128)(2,1)S(1)}, f32[1024,384]{1,0:T(8,128)S(1)}, f32[4,384]{1,0:T(4,128)S(1)}, f32[2,96,2304]{2,1,0:T(8,128)S(1)}, bf16[2,3,...) custom-call(bf16[1024,384]{1,0:T(8,128)(2,1)} %bitcast.8, ...), custom_call_target="tpu_custom_call" | custom-call | tf_op jit(solution)/shard_map/blocks/pallas_call | solution.py:947
  114.2 3.2 %finish.1 = (bf16[1024,384]{1,0:T(8,128)(2,1)}, f32[1024,384]{1,0:T(8,128)}, f32[4,384]{1,0:T(4,128)}, f32[2,96,2304]{2,1,0:T(8,128)}, f32[2,96,1152]{2,1,0:T(8,...) custom-call(bf16[1024,384]{1,0:T(8,128)(2,1)S(1)} %get-tuple-element.23.refs_0_, ...), custom_call_target="tpu_custom_call" | custom-call | tf_op jit(solution)/shard_map/finish/pallas_call | solution.py:970

commit v2 on v1

--- a/solution.py
+++ b/solution.py
@@ -18,13 +18,13 @@
 GELU_A = 0.7978845608028654
 GELU_B = GELU_A * 0.044715
 KINDS = ("u", "d", "q0", "q1", "q2")
-SPLIT = ((0, "d"), (1, "d"))
-DIRECT = ((0, "d"), (0, "q"), (0, "u"), (1, "d"))
+SPLIT = ((0, "q"), (1, "d"))
+DIRECT = ((0, "d"), (0, "q"), (1, "d"), (1, "u"))
 STEPS = ()
-ONE = ((0, "q1"),)
+ONE = ((0, "q2"),)
 METHOD = (
-    {"u": "q", "d": "steps", "q0": "ring", "q1": "steps", "q2": "q"},
-    {"u": "q", "d": "q", "q0": "steps", "q1": "steps", "q2": "q"},
+    {"u": "ring", "d": "steps", "q0": "steps", "q1": "q", "q2": "q"},
+    {"u": "q", "d": "q", "q0": "q", "q1": "q", "q2": "q"},
 )
 
 
@@ -221,6 +221,44 @@
         n = local_index.setdefault(key, len(local_index))
         return pltpu.make_async_copy(src, dst, local_sems.at[n])
 
+    def loads(what):
+        if what == "c":
+            return [local(("cd",), inp.cond, k.cd)]
+        if what == "a":
+            return [local(("wa",), inp.ada, k.wa)]
+        if what == "u":
+            return [local(("wu",), inp.up_w, k.wu.at[:, f])]
+        if what == "d":
+            return [local(("wd",), inp.down_w, k.wd.at[:, f])]
+        if what == "t":
+            return [local(("tk",), inp.tokens, k.da), local(("db",), inp.cotangent, k.db)]
+        return [
+            local(
+                ("wq", n, p),
+                inp.qkv_w.at[:, :, :, pl.ds(n * D + p * W, W)],
+                k.wq.at[:, f, :, :, pl.ds(p * D + n * W, W)],
+            )
+            for n in range(3)
+            for p in range(PAIRS)
+        ] + [local(("wp",), inp.proj_w, k.wq.at[:, f, :, :, pl.ds(3 * D, D)])]
+
+    def load(what):
+        for copy in loads(what):
+            copy.start()
+
+    arrived = set()
+
+    def loaded(what):
+        if what not in arrived:
+            arrived.add(what)
+            for copy in loads(what):
+                copy.wait()
+
+    def tokens_ready():
+        loaded("t")
+        for i in images:
+            k.xs[0, rows(i), :] = k.da[rows(i), :].astype(f32)
+
     whole = {"q": k.wq, "u": k.wu, "d": k.wd}
 
     def main(b, w):
@@ -246,6 +284,7 @@
         return k.wd.at[b, pl.ds(0, n), :, 0, rest] if w == "d" else whole[w].at[b, pl.ds(0, n), 0, rest]
 
     def w_z(b, w):
+        loaded(w)
         for r in (1, 3, 2) if (b, w) in DIRECT else (1, 3):
             p = w_main(b, w, f)
             send(("wz", b, w), p, p, at_z(r))
@@ -338,6 +377,7 @@
     tiles = ((0, 1), (1, 3))
 
     def mod_partial(part):
+        loaded("a")
         a = dot(k.cz[...].reshape(F * 16, D), cols().astype(bf))
         masked = [(a * tile_mask(F * 16, p)).astype(bf) for p in range(4)]
         lo, hi = tiles[part]
@@ -779,57 +819,44 @@
         pl.when(me >= 0)(functools.partial(run, *todo))
 
     barrier = pltpu.get_barrier_semaphore()
-    everyone = [at_q(j, r) for r in range(F) for j in range(4)][1:] + [at_c(j) for j in range(4)]
+    everyone = [at_z(r) for r in range(1, F)] + [at_q(j) for j in range(1, 4)] + [at_c(j) for j in range(4)]
     for peer in everyone:
         pl.semaphore_signal(barrier, inc=1, device_id=peer, device_id_type=MESH)
-    cond_load = local(("cd",), inp.cond, k.cd)
-    cond_load.start()
-    ada_load = local(("wa",), inp.ada, k.wa)
-    w_loads = {"q": [], "u": [local(("wu",), inp.up_w, k.wu.at[:, f])], "d": [local(("wd",), inp.down_w, k.wd.at[:, f])]}
-    for which in range(3):
-        for p in range(PAIRS):
-            w_loads["q"].append(
-                local(
-                    ("wq", which, p),
-                    inp.qkv_w.at[:, :, :, pl.ds(which * D + p * W, W)],
-                    k.wq.at[:, f, :, :, pl.ds(p * D + which * W, W)],
-                )
-            )
-    w_loads["q"].append(local(("wp",), inp.proj_w, k.wq.at[:, f, :, :, pl.ds(3 * D, D)]))
-    other_loads = [local(("tk",), inp.tokens, k.da), local(("db",), inp.cotangent, k.db)]
-    for copy in w_loads["q"] + [ada_load] + w_loads["u"] + w_loads["d"] + other_loads:
-        copy.start()
-    cond_load.wait()
+    load("c")
+    load("q")
+    load("a")
+    load("u")
+    load("d")
+    load("t")
+    loaded("c")
     cond_tile()
-    for copy in w_loads["q"] + [ada_load] + w_loads["u"] + w_loads["d"] + other_loads:
-        copy.wait()
-    for i in images:
-        k.xs[0, rows(i), :] = k.da[rows(i), :].astype(f32)
+    loaded("q")
     pl.semaphore_wait(barrier, len(everyone))
 
-    run((cond_z,), (w_z, 1, "q"), (w_z, 0, "q"), (wait, "recv", ("cz",), k.cz.at[pl.ds(0, F - 1)]), (w_z, 0, "u"), (mod_partial, 0), (w_z, 0, "d"), (w_relay, 1, "q"), (cond_zq,), (w_zq, 0, "q"), (w_zq, 0, "u"), (w_z, 1, "u"), (mod_ready, 0))
+    run((cond_z,), (w_z, 0, "u"), (w_z, 0, "q"), (wait, "recv", ("cz",), k.cz.at[pl.ds(0, F - 1)]), (w_z, 1, "q"), (cond_zq,), (w_relay, 0, "u"), (w_z, 0, "d"), (w_zq, 0, "q"), (w_relay, 0, "q"), (mod_partial, 0), (w_relay, 1, "q"), (w_opposite, 0, "u"), (w_z, 1, "u"), (mod_partial, 1), (w_qc, 0, "q"), (w_zq, 0, "d"), (w_z, 1, "d"), (mod_ready, 0))
+    tokens_ready()
 
     def forward(step, _):
         b = step
         phase((each, fwd_norm, b),)
-        at_block(b, 0, (w_zq, 0, "d"), (w_relay, 0, "d"), (w_qc, 0, "q"), (mod_partial, 1), (w_opposite, 1, "q"), (w_ready, 0, "q"))
+        at_block(b, 0, (w_opposite, 1, "q"), (w_ready, 0, "q"))
         phase((each, fwd_qkv, b),)
-        at_block(b, 0, (w_relay, 1, "u"), (w_z, 1, "d"))
+        at_block(b, 0, (cond_qc,), (w_qc, 0, "u"))
         at_block(b, 1, (w_qc, 1, "u"),)
         at_block(b, 1, (keep_wait, "pt"),)
         phase((each, fwd_probs, b), (each, fwd_mix, b))
         at_block(b, 0, (keep_start, "pt"))
-        at_block(b, 0, (w_qc, 0, "u"), (mod_ready, 1))
+        at_block(b, 0, (w_zq, 1, "u"), (cond_ready,), (w_ready, 0, "u"), (mod_ready, 1))
         phase((each, fwd_proj, b),)
-        at_block(b, 0, (w_ready, 0, "u"), (w_qc, 0, "d"), (w_opposite, 1, "u"))
-        at_block(b, 1, (w_ready, 1, "u"),)
+        at_block(b, 0, (w_qc, 0, "d"),)
+        at_block(b, 1, (w_ready, 1, "u"), (w_qc, 1, "d"))
         at_block(b, 1, (keep_wait, "hid"), (keep_wait, "act"))
         phase((fwd_up, b),)
         at_block(b, 0, (keep_start, "hid"), (keep_start, "act"))
-        at_block(b, 0, (w_qc, 1, "q"), (w_ready, 0, "d"), (w_zq, 1, "d"))
-        at_block(b, 1, (w_qc, 1, "d"), (w_ready, 1, "d"))
+        at_block(b, 0, (w_qc, 1, "q"), (w_ready, 0, "d"), (w_zq, 1, "d"), (w_relay, 1, "d"))
+        at_block(b, 1, (w_ready, 1, "d"),)
         phase((fwd_down, b),)
-        at_block(b, 0, (w_relay, 1, "d"), (w_ready, 1, "q"))
+        at_block(b, 0, (w_ready, 1, "q"),)
         return 0
 
     lax.fori_loop(0, B, forward, 0)
@@ -841,41 +868,40 @@
         b = B - 1 - step
         at_block(b, 0, (fetch_wait, "hid"))
         phase((bwd_hidden, b),)
-        at_block(b, 0, (dm_zq, 1),)
         phase((grad_up, b),)
         at_block(b, 1, (g_c, 1, "u"),)
-        at_block(b, 0, (g_c, 0, "u"), (g_fly, 1, "q0"), (g_3, 1, "u"), (g_2, 1, "d"))
+        at_block(b, 0, (g_c, 0, "u"), (g_2, 1, "d"), (g_3, 1, "u"), (g_2, 1, "q0"))
         at_block(b, 0, (fetch_wait, "act"))
         phase((grad_down, b),)
         at_block(b, 1, (g_c, 1, "d"), (g_1, 1, "u"))
-        at_block(b, 0, (g_c, 0, "d"), (g_1, 0, "u"), (g_fly, 1, "q1"))
+        at_block(b, 0, (g_c, 0, "d"), (g_1, 0, "u"), (dm_qc, 1))
         at_block(b, B - 1, (out_wait,))
         phase((bwd_second, b),)
         at_block(b, 1, (fetch_start, "hid"))
         at_block(b, 1, (g_1, 1, "d"), (dm_start, 1))
-        at_block(b, 0, (g_1, 0, "d"), (dm_start, 0), (g_2, 1, "q0"))
+        at_block(b, 0, (g_2, 1, "q1"), (g_1, 0, "d"), (dm_start, 0), (dm_ready, 1))
         phase((grad_proj, b),)
         at_block(b, 0, (fetch_wait, "pt"))
         phase((bwd_heads, b, 0),)
-        at_block(b, 0, (g_4, 1, "u"),)
+        at_block(b, 0, (g_3, 1, "d"), (g_2, 1, "q2"), (g_3, 1, "q0"))
         phase((grad_qkv, b, 0),)
         at_block(b, 1, (g_c, 1, "q0"),)
         at_block(b, 0, (g_c, 0, "q0"),)
         phase((bwd_heads, b, 1),)
         at_block(b, 1, (g_1, 1, "q0"),)
-        at_block(b, 0, (g_1, 0, "q0"), (g_5, 1, "u"))
+        at_block(b, 0, (g_ring, 0, "u"), (g_1, 0, "q0"))
         phase((grad_qkv, b, 1),)
-        at_block(b, 1, (g_c, 1, "q1"),)
-        at_block(b, 0, (g_c, 0, "q1"),)
+        at_block(b, 1, (g_c, 1, "q1"), (dm_zq, 1))
+        at_block(b, 0, (g_c, 0, "q1"), (g_fly, 0, "d"), (g_3, 1, "q1"))
         phase((bwd_heads, b, 2),)
         at_block(b, 1, (fetch_start, "pt"), (fetch_start, "act"))
         at_block(b, 1, (g_1, 1, "q1"), (g_2, 1, "u"))
-        at_block(b, 0, (g_1, 0, "q1"), (g_3, 1, "d"), (g_2, 0, "u"), (g_3, 1, "q0"), (g_2, 1, "q1"))
+        at_block(b, 0, (g_4, 1, "d"), (g_1, 0, "q1"), (g_4, 1, "q0"), (dm_zq, 0))
         phase((grad_qkv, b, 2),)
         at_block(b, 1, (g_c, 1, "q2"),)
         at_block(b, 0, (g_c, 0, "q2"),)
         phase((bwd_first, b, images[: I // 2]),)
-        at_block(b, 0, (g_fly, 0, "d"), (g_ring, 0, "q0"), (g_1, 0, "q2"))
+        at_block(b, 0, (g_fly, 0, "q0"), (g_5, 1, "d"), (g_5, 1, "q0"))
         phase((bwd_first, b, images[I // 2 :]),)
         at_block(b, 1, (g_1, 1, "q2"),)
         return 0
@@ -884,7 +910,7 @@
     run((dm_start, 2),)
     g_load = local(("g",), k.xs.at[B], out.grad_tokens)
     g_load.start()
-    run((g_fly, 0, "q1"), (cond_qc,), (g_2, 1, "q2"), (dm_qc, 1), (dm_zq, 0), (g_4, 1, "d"), (g_4, 1, "q0"), (cond_ready,), (dm_ready, 1), (grad_ada, 1), (g_5, 1, "d"), (g_5, 1, "q0"), (g_2, 0, "d"), (g_3, 0, "u"), (g_3, 1, "q1"), (g_2, 0, "q2"), (g_2, 0, "q1"), (g_2, 0, "q0"), (dm_zq, 2), (dcond_send,), (dm_qc, 0), (g_3, 1, "q2"), (g_4, 0, "u"), (dm_ready, 0), (grad_ada, 0), (g_4, 1, "q1"), (g_3, 0, "q0"), (g_5, 0, "u"), (g_3, 0, "d"), (g_5, 1, "q1"), (g_3, 0, "q2"), (dm_qc, 2), (g_4, 1, "q2"), (g_3, 0, "q1"), (dm_ready, 2), (grad_ada, 2), (g_4, 0, "q0"), (g_5, 1, "q2"), (dcond_finish,), (g_5, 0, "q0"), (g_4, 0, "d"), (g_4, 0, "q2"), (g_5, 0, "d"), (all_sent,), (g_5, 0, "q1"), (g_5, 0, "q2"), (all_sent,))
+    run((g_1, 0, "q2"), (g_4, 1, "q1"), (g_2, 0, "d"), (grad_ada, 1), (g_4, 1, "u"), (g_3, 1, "q2"), (g_5, 1, "q1"), (g_2, 0, "q1"), (g_5, 1, "u"), (g_2, 0, "u"), (dm_qc, 0), (g_2, 0, "q0"), (dm_zq, 2), (dcond_send,), (dm_ready, 0), (grad_ada, 0), (g_2, 0, "q2"), (g_4, 1, "q2"), (g_3, 0, "d"), (g_5, 1, "q2"), (g_3, 0, "u"), (g_3, 0, "q1"), (g_3, 0, "q0"), (dm_qc, 2), (dcond_finish,), (g_3, 0, "q2"), (dm_ready, 2), (grad_ada, 2), (g_4, 0, "d"), (g_4, 0, "u"), (g_5, 0, "d"), (g_4, 0, "q1"), (g_4, 0, "q0"), (g_5, 0, "u"), (g_5, 0, "q1"), (all_sent,), (g_5, 0, "q2"), (g_5, 0, "q0"), (all_sent,))
     g_load.wait()
     local(("grad_cond",), k.gc.at[pl.ds(0, I)], out.grad_cond).wait()
     for b in range(B):

time: 118 us -> 114 us (0.966)
  Pallas kernels: 117 us -> 113 us
    pallas_call x1, Pallas kernels: 114 us -> 110 us  [body(): pl.pallas_call(functools.partial(kernel, names, F, I, L, D, FF, B), name=...]
where the time goes in v2:
time: 114 us
  Pallas kernels  113 us (99%)
    pallas_call x1, Pallas kernels, body(): pl.pallas_call(functools.partial(kernel, names, F, I, L, D, FF, B), name=...  110 us
    pallas_call x1, Pallas kernels, body(): pl.pallas_call(finish, name='finish', out_shape=results[:4] + [jax.ShapeD...  3.18 us

profile of v2, /device:TPU:0, one launch (start us, length us, event | category | flops | bytes accessed | tf_op | source)
XLA Modules:
  0.0 113.6 jit_solution(13214775599481664279)
XLA Ops:
  0.6 109.6 %blocks.1 = (bf16[1024,384]{1,0:T(8,128)(2,1)S(1)}, f32[1024,384]{1,0:T(8,128)S(1)}, f32[4,384]{1,0:T(4,128)S(1)}, f32[2,96,2304]{2,1,0:T(8,128)S(1)}, bf16[2,3,...) custom-call(bf16[1024,384]{1,0:T(8,128)(2,1)} %bitcast.8, ...), custom_call_target="tpu_custom_call" | custom-call | tf_op jit(solution)/shard_map/blocks/pallas_call | solution.py:973
  110.2 3.2 %finish.1 = (bf16[1024,384]{1,0:T(8,128)(2,1)}, f32[1024,384]{1,0:T(8,128)}, f32[4,384]{1,0:T(4,128)}, f32[2,96,2304]{2,1,0:T(8,128)}, f32[2,96,1152]{2,1,0:T(8,...) custom-call(bf16[1024,384]{1,0:T(8,128)(2,1)S(1)} %get-tuple-element.23.refs_0_, ...), custom_call_target="tpu_custom_call" | custom-call | tf_op jit(solution)/shard_map/finish/pallas_call | solution.py:996

commit v3 on v2

--- a/solution.py
+++ b/solution.py
@@ -80,6 +80,8 @@
         mt=((B, D, T), bf),
         att=((B, T, D), bf),
         mid=((B, T, D), f32),
+        r1=((B, T, 1), f32),
+        r2=((B, T, 1), f32),
         si=((B, T, D), bf),
         hid=((T, FF), bf),
         br=((B, T, D), bf),
@@ -631,7 +633,10 @@
         return slice(p * D + which * W, p * D + (which + 1) * W)
 
     def fwd_norm(b, i):
-        hat, _ = norm_hat(state(b, i))
+        x = state(b, i)
+        hat, k.r1[b, rows(i), :] = norm_hat(x)
+        k.xs[b, rows(i), :] = hat
+        k.xs[b + 1, rows(i), :] = x
         k.fi[b, rows(i), :] = (hat * (1.0 + piece(b, i, 1)) + piece(b, i, 0)).astype(bf)
 
     def fwd_qkv(b, i):
@@ -666,9 +671,10 @@
         r = rows(i)
         att = dot(k.mt[b, :, r], m_proj(b), TN)
         k.att[b, r, :] = att.astype(bf)
-        mid = state(b, i) + piece(b, i, 2) * att
-        k.mid[b, r, :] = mid
-        hat, _ = norm_hat(mid)
+        mid = state(b + 1, i) + piece(b, i, 2) * att
+        k.xs[b + 1, r, :] = mid
+        hat, k.r2[b, r, :] = norm_hat(mid)
+        k.mid[b, r, :] = hat
         k.si[b, r, :] = (hat * (1.0 + piece(b, i, 4)) + piece(b, i, 3)).astype(bf)
 
     def fwd_up(b):
@@ -685,7 +691,7 @@
         k.br[b] = acc.astype(bf)
         for i in images:
             r = rows(i)
-            k.xs[b + 1, r, :] = k.mid[b, r, :] + piece(b, i, 5) * acc[r]
+            k.xs[b + 1, r, :] = k.xs[b + 1, r, :] + piece(b, i, 5) * acc[r]
 
     def turn():
         for i in images:
@@ -712,7 +718,7 @@
         for i in images:
             r = rows(i)
             d = acc[r]
-            hat, rs = norm_hat(k.mid[b, r, :])
+            hat, rs = k.mid[b, r, :], k.r2[b, r, :]
             dm_row(b, i, 3, jnp.sum(d, axis=0, keepdims=True))
             dm_row(b, i, 4, jnp.sum(d * hat, axis=0, keepdims=True))
             d_mid = k.xs[B, r, :] + norm_back(d * (1.0 + piece(b, i, 4)), hat, rs)
@@ -778,7 +784,7 @@
         for i in some:
             r = rows(i)
             d = dot(k.qkv[b, r, :], m_qkv(b), NT)
-            hat, rs = norm_hat(state(b, i))
+            hat, rs = state(b, i), k.r1[b, r, :]
             dm_row(b, i, 0, jnp.sum(d, axis=0, keepdims=True))
             dm_row(b, i, 1, jnp.sum(d * hat, axis=0, keepdims=True))
             k.xs[B, r, :] = k.xs[B, r, :] + norm_back(d * (1.0 + piece(b, i, 1)), hat, rs)
@@ -979,7 +985,7 @@
         scratch_shapes=[pltpu.VMEM(*shapes[n]) for n in names]
         + [pltpu.SemaphoreType.DMA((N_SEMS,)), pltpu.SemaphoreType.DMA((N_LOCAL,))],
         compiler_params=pltpu.CompilerParams(
-            collective_id=0, has_side_effects=True, vmem_limit_bytes=56 * 2**20 + 2**19
+            collective_id=0, has_side_effects=True, vmem_limit_bytes=57 * 2**20
         ),
     )(
         tokens.reshape(T, D),

time: 114 us -> 114 us (level)
  no operation moved by 1% of the time
where the time goes in v3:
time: 114 us
  Pallas kernels  113 us (99%)
    pallas_call x1, Pallas kernels, body(): pl.pallas_call(functools.partial(kernel, names, F, I, L, D, FF, B), name=...  110 us
    pallas_call x1, Pallas kernels, body(): pl.pallas_call(finish, name='finish', out_shape=results[:4] + [jax.ShapeD...  3.18 us

profile of v3, /device:TPU:0, one launch (start us, length us, event | category | flops | bytes accessed | tf_op | source)
XLA Modules:
  0.0 113.7 jit_solution(6063934942778350676)
XLA Ops:
  0.6 109.7 %blocks.1 = (bf16[1024,384]{1,0:T(8,128)(2,1)S(1)}, f32[1024,384]{1,0:T(8,128)S(1)}, f32[4,384]{1,0:T(4,128)S(1)}, f32[2,96,2304]{2,1,0:T(8,128)S(1)}, bf16[2,3,...) custom-call(bf16[1024,384]{1,0:T(8,128)(2,1)} %bitcast.8, ...), custom_call_target="tpu_custom_call" | custom-call | tf_op jit(solution)/shard_map/blocks/pallas_call | solution.py:979
  110.3 3.2 %finish.1 = (bf16[1024,384]{1,0:T(8,128)(2,1)}, f32[1024,384]{1,0:T(8,128)}, f32[4,384]{1,0:T(4,128)}, f32[2,96,2304]{2,1,0:T(8,128)}, f32[2,96,1152]{2,1,0:T(8,...) custom-call(bf16[1024,384]{1,0:T(8,128)(2,1)S(1)} %get-tuple-element.23.refs_0_, ...), custom_call_target="tpu_custom_call" | custom-call | tf_op jit(solution)/shard_map/finish/pallas_call | solution.py:1002
